TPU v7x, 32 devices: a whole 2x2x4 slice. The times are simulated.
32 devices in a mesh: snp: 2 (over y), samp: 16 (over z, x, core).
Axes of the slice: x: 2, y: 2, z: 4, core: 2. Of those that a mesh axis runs over, the one named last changes fastest.
Arguments:
- dosages: bfloat16 [12288, 1024], P('samp', 'snp'), may hold values from 0 to 2
- residual: float32 [12288], P('samp'), may hold values from -40 to 40
- pair_list: int32 [4, 2], replicated, may hold values from 0 to 3, as said below
- block_slot: int32 [4], replicated, may hold values from 0 to 3, as said below
- pair_counts: int32 [4], replicated, may hold values from 3072 to 12288, as said below
Outputs:
- epistasis_score: float32 [1024], P('snp')
Inputs may be any that keep to these rules, and one draw needn't show every extreme that they name: `pair_list`: block b is paired with block (b + 1) mod 4, each such pair listed once, in some order and orientation. Counting each pair at the snp group block_slot[first block] // 2, no group gets more than 4 pairs and one group gets exactly 4. A permutation: block b is stored in columns block_slot[b] * 256 onward, on snp group block_slot[b] // 2. Pair p uses the samples with index below pair_counts[p]; some pair uses all 12288.
All inputs are finite; a program needn't handle non-finite values.
Results may differ from a plain program's by a relative error of at most 0.0021.
Values may be sent and summed in bfloat16 or wider, within the bound.
A program may use at most 64 MiB of HBM per device.

v0:
```python
import math
import jax
import jax.numpy as jnp
from jax import lax
from jax.sharding import PartitionSpec as P

BLOCK = 256


def on_device(dosages, residual, pair_list, block_slot, pair_counts):
    local_rows = dosages.shape[0]
    groups = lax.axis_size("snp")
    shards = lax.axis_size("samp")
    total_rows = local_rows * shards
    blocks = block_slot.shape[0]
    num_pairs = pair_list.shape[0]
    highest = lax.Precision.HIGHEST
    gathered = lax.all_gather(dosages, "snp", axis=1, tiled=True)
    spread_sum = lax.psum(jnp.sum(residual * residual), "samp")
    spread_var = spread_sum / total_rows
    position = lax.axis_index("samp") * local_rows + jnp.arange(local_rows, dtype=jnp.int32)
    block_ids = jnp.arange(blocks, dtype=jnp.int32)
    slot_first = jnp.sum(
        (pair_list[:, 0:1] == block_ids[None, :]).astype(jnp.int32) * block_slot[None, :], axis=1
    )
    slot_second = jnp.sum(
        (pair_list[:, 1:2] == block_ids[None, :]).astype(jnp.int32) * block_slot[None, :], axis=1
    )
    group_id = lax.axis_index("snp")
    pair_ids = jnp.arange(num_pairs, dtype=jnp.int32)
    width_slots = (num_pairs + groups - 1) // groups
    wanted = group_id * width_slots + jnp.arange(width_slots, dtype=jnp.int32)
    picked = (pair_ids[:, None] == wanted[None, :]).astype(jnp.int32)
    live_slot = jnp.sum(picked, axis=0)
    first_at = jnp.sum(picked * slot_first[:, None], axis=0)
    second_at = jnp.sum(picked * slot_second[:, None], axis=0)
    count_at = jnp.sum(picked * pair_counts[:, None], axis=0)
    live_rows = (position[None, :] < count_at[:, None]).astype(jnp.float32) * live_slot[
        :, None
    ].astype(jnp.float32)
    weight_rows = residual[None, :] * live_rows

    def masked_block(operand):
        second_slot, live = operand
        right = lax.dynamic_slice_in_dim(gathered, second_slot * BLOCK, BLOCK, 1)
        right_sq = right * right
        return (right_sq.astype(jnp.float32) * live[:, None]).astype(jnp.bfloat16)

    masked = lax.map(masked_block, (second_at, live_rows))
    rows = BLOCK // shards

    def one_slot(slot, buffer):
        first_col = lax.dynamic_index_in_dim(first_at, slot, 0, keepdims=False) * BLOCK
        second_col = lax.dynamic_index_in_dim(second_at, slot, 0, keepdims=False) * BLOCK
        left = lax.dynamic_slice_in_dim(gathered, first_col, rows * lax.axis_size("samp"), 1)
        right = lax.dynamic_slice_in_dim(gathered, second_col, BLOCK, 1)
        row_weight = lax.dynamic_index_in_dim(weight_rows, slot, 0, keepdims=False)
        masked_slot = lax.dynamic_index_in_dim(masked, slot, 0, keepdims=False)
        weighted = (left.astype(jnp.float32) * row_weight[:, None]).astype(jnp.bfloat16)
        left_sq = left * left
        cross = jnp.einsum("si,sj->ij", weighted, right, preferred_element_type=jnp.float32)
        moment = jnp.einsum("si,sj->ij", left_sq, masked_slot, preferred_element_type=jnp.float32)
        stacked = jnp.stack([cross, moment], axis=1)[:, :, None, :]
        return lax.dynamic_update_slice_in_dim(buffer, stacked, slot, 2)

    start_buffer = jnp.zeros((rows * lax.axis_size("samp"), 2, width_slots, BLOCK), jnp.float32)
    shares = lax.psum_scatter(
        lax.fori_loop(0, width_slots, one_slot, start_buffer),
        "samp",
        scatter_dimension=0,
        tiled=True,
    )
    zvalue = shares[:, 0] / jnp.sqrt(spread_var * shares[:, 1] + 1e-06)
    row_sums = jnp.sum(zvalue, axis=2)
    col_sums = jnp.sum(zvalue, axis=0)
    live_float = live_slot.astype(jnp.float32)
    first_hot = (first_at[:, None] == block_ids[None, :]).astype(jnp.float32) * live_float[:, None]
    second_hot = (second_at[:, None] == block_ids[None, :]).astype(jnp.float32) * live_float[
        :, None
    ]
    by_column = jnp.dot(second_hot.T, col_sums, precision=highest)
    by_row = jnp.dot(first_hot.T, row_sums.T, precision=highest)
    row_start = lax.axis_index("samp") * rows
    placed = lax.dynamic_update_slice_in_dim(
        jnp.zeros((blocks, BLOCK), jnp.float32), by_row, row_start, 1
    )
    partial_scores = (by_column + placed).reshape(blocks * BLOCK)
    group_part = lax.psum_scatter(partial_scores, "snp", scatter_dimension=0, tiled=True)
    totals = lax.psum(group_part, "samp")
    return totals / math.sqrt(2 * BLOCK)


def solution(mesh):
    return jax.shard_map(
        on_device,
        mesh=mesh,
        in_specs=(P("samp", "snp"), P("samp"), P(), P(), P()),
        out_specs=P("snp"),
        check_vma=False,
    )
```

profile of v0, /device:TPU:0, one launch (start us, length us, event | category | flops | bytes accessed | tf_op | source)
XLA Modules:
  0.0 156.7 jit_solution(12194418596713878061)
XLA Ops:
  6.5 0.7 all-gather.2.cloned.1.call-update
  7.3 0.8 slice_bitcast_fusion
  8.1 0.9 select_reduce_fusion.1
  9.0 0.9 select_reduce_fusion.4
  9.9 0.8 compare_select_fusion
  10.6 28.2 %all-gather.2.cloned.1.call-done = bf16[768,1024]{1,0:T(8,128)(2,1)} async-done(((bf16[768,512]{1,0:T(8,128)(2,1)}), bf16[768,1024]{1,0:T(8,128)(2,1)}) %all-gather.2.cloned.1.call-update) | async-done | bytes 1572880 | tf_op jit(solution)/shard_map/all_gather | solution.py:18
  38.8 4.9 %while.23 = (s32[]{:T(128)}, bf16[2,768,256]{2,1,0:T(8,128)(2,1)S(1)}, s32[2]{0:T(128)S(1)}, bf16[768,1024]{1,0:T(8,128)(2,1)}, f32[2,768]{1,0:T(2,128)S(1)}, /*...) while((s32[]{:T(128)}, bf16[2,768,256]{2,1,0:T(8,128)(2,1)S(1)}, s32[2]{0:T(128)S(1)}, ...), condition=%wide.region_7.0_spmd, body=%wide.region_6.0_spmd.sunk | while | flops 983046 | bytes 796835 | solution.py:49
  40.1 1.2 fusion.35
  41.3 0.6 dynamic_slice.85
  42.5 1.2 fusion.35
  43.8 11.0 %while.24 = (s32[]{:T(128)}, f32[256,2,2,256]{3,0,1,2:T(8,128)S(1)}, s32[2]{0:T(128)S(1)}, bf16[768,1024]{1,0:T(8,128)(2,1)}, f32[2,768]{1,0:T(2,128)S(1)}, /*in...) while((s32[]{:T(128)}, ...), condition=%wide.region_9.10_spmd, body=%wide.region_8.9_spmd.sunk | while | flops 202637312 | bytes 3155701 | solution.py:68
  43.8 0.6 dynamic_slice.91
  45.0 0.6 dynamic_slice.92
  46.3 1.6 %convolution_bitcast_fusion.5 = f32[256,1,256]{2,0,1:T(8,128)S(1)} fusion(bf16[768,1024]{1,0:T(8,128)(2,1)} %get-tuple-element.320, s32[]{:T(128)S(6)} %select_n.38, f32[768]{0:T(1024)S(1)} %dynamic-slice_reduce_fusion.5, s32[]{:T(128)S(6)} %select_n.37), kind=kOutput, calls=%fused_computation.5.clone.1 | convolution fusion | flops 101253120 | bytes 1051656 | tf_op jit(solution)/shard_map/while/body/eval_jaxpr/si,sj->ij/dot_general | solution.py:61
  47.9 1.3 convolution_bitcast_fusion.4
  50.5 0.6 dynamic_slice.92
  51.7 1.6 %convolution_bitcast_fusion.5 = f32[256,1,256]{2,0,1:T(8,128)S(1)} fusion(bf16[768,1024]{1,0:T(8,128)(2,1)} %get-tuple-element.320, s32[]{:T(128)S(6)} %select_n.38, f32[768]{0:T(1024)S(1)} %dynamic-slice_reduce_fusion.5, s32[]{:T(128)S(6)} %select_n.37), kind=kOutput, calls=%fused_computation.5.clone.1 | convolution fusion | flops 101253120 | bytes 1051656 | tf_op jit(solution)/shard_map/while/body/eval_jaxpr/si,sj->ij/dot_general | solution.py:61
  53.3 1.3 convolution_bitcast_fusion.4
  54.7 1.0 copy-done
  56.3 33.9 %psum.14 = f32[]{:T(128)} all-reduce(f32[]{:T(128)} %multiply_reduce_fusion), channel_id=1, replica_groups=mesh['snp'=2,'samp'=16] {'samp'}, use_global_device_ids=true, to_apply=%region_12.13 | all-reduce | flops 1 | bytes 8 | tf_op jit(solution)/shard_map/psum | solution.py:19
  92.1 21.1 %reduce-scatter.2.cloned.1.call-done = f32[16,2,2,256]{3,0,1,2:T(8,128)} async-done(((f32[256,2,2,256]{3,0,1,2:T(8,128)}), f32[16,2,2,256]{3,0,1,2:T(8,128)}) %reduce-scatter.2.cloned.1.call-update) | async-done | bytes 65552 | tf_op jit(solution)/shard_map/reduce_scatter | solution.py:67
  113.3 0.9 fusion.15
  114.8 4.9 %all-reduce = f32[1024]{0:T(1024)S(1)} all-reduce(f32[1024]{0:T(1024)S(1)} %bitcast.43), channel_id=3, replica_groups=mesh['snp'=2,'samp'=16] {'snp'}, use_global_device_ids=true, to_apply=%region_15.16.clone | all-reduce | flops 1024 | bytes 8192
  119.8 29.5 %psum.15 = f32[512]{0:T(512)S(1)} all-reduce(f32[512]{0:T(512)S(1)} %dynamic-slice.2), channel_id=1, replica_groups=mesh['snp'=2,'samp'=16] {'samp'}, use_global_device_ids=true, to_apply=%region_16.17 | all-reduce | flops 512 | bytes 4096 | tf_op jit(solution)/shard_map/psum | solution.py:89
  (29 shorter events, 4.0 us)
Async XLA Ops:
  6.5 32.3 %all-gather.2.cloned.1.call-start = ((), (), s32[]{:S(2)}) async-start(), calls=%async_computation.1 | async-start | bytes 2359296 | tf_op jit(solution)/shard_map/all_gather | solution.py:18
  7.3 106.0 %reduce-scatter.2.cloned.1.call-start = ((), (), s32[]{:S(2)}) async-start(), calls=%async_computation.2 | async-start | bytes 1114112 | tf_op jit(solution)/shard_map/reduce_scatter | solution.py:67
  43.7 12.0 %copy-start.1 = (f32[768]{0:T(1024)S(1)}, f32[768]{0:T(1024)}, u32[]{:S(2)}) copy-start(f32[768]{0:T(1024)} %param.10) | copy-start | bytes 9220
  43.7 47.1 %copy-start.2 = (u32[32]{0:T(128)S(1)}, u32[32]{0:T(128)}, u32[]{:S(2)}) copy-start(u32[32]{0:T(128)} %constant.108) | copy-start | bytes 388
  54.7 1.0 copy-start
Sparse Core Ops, SparseCore 0:
  8.9 29.8 all-gather.1
  55.9 57.3 reduce-scatter.1
where the time goes:
time: 157 us
  blocking collectives  68.3 us (44%)
  waiting for transfers between devices  50.1 us (32%)
  between operations  14.8 us (9%)
  other arithmetic  7 us (4%)
  matrix products  6.34 us (4%)
  local copies, waits for them, and re-layouts  6.29 us (4%)
  loops' own time  3.83 us (2%)
    psum x1, blocking collectives, on_device(): spread_sum = lax.psum(jnp.sum(residual * residual), 'samp')  33.9 us
    psum x1, blocking collectives, on_device(): totals = lax.psum(group_part, 'samp')  29.5 us
    all_gather x1, waiting for transfers between devices, on_device(): gathered = lax.all_gather(dosages, 'snp', axis=1, tiled=True)  28.2 us
    reduce_scatter x1, waiting for transfers between devices, on_device(): lax.psum_scatter(lax.fori_loop(0, width_slots, one_slot, start_buffer), '...  21.1 us
    unnamed x1, blocking collectives  4.95 us
    dot_general x2, matrix products, one_slot(): jnp.einsum('si,sj->ij', weighted, right, preferred_element_type=jnp.float32)  3.19 us
  transfers between devices with their start and end apart: 2, of which 2 were waited for; matrix products, arithmetic and copies ran while one was open for 3% of the time, Pallas kernels for 0%

commit v1 on v0

--- a/solution.py
+++ b/solution.py
@@ -86,7 +86,7 @@
     )
     partial_scores = (by_column + placed).reshape(blocks * BLOCK)
     group_part = lax.psum_scatter(partial_scores, "snp", scatter_dimension=0, tiled=True)
-    totals = lax.psum(group_part, "samp")
+    totals = jnp.sum(lax.all_gather(group_part, "samp"), axis=0)
     return totals / math.sqrt(2 * BLOCK)
 
 

time: 157 us -> 147 us (0.936)
  blocking collectives: 68.3 us -> 58.4 us
    psum x1 -> x0, blocking collectives: 29.5 us -> none  [on_device(): totals = lax.psum(group_part, 'samp')]
    all_gather x0 -> x1, blocking collectives: none -> 19.6 us  [on_device(): totals = jnp.sum(lax.all_gather(group_part, 'samp'), axis=0)]
where the time goes in v1:
time: 147 us
  blocking collectives  58.4 us (40%)
  waiting for transfers between devices  50.1 us (34%)
  between operations  14.8 us (10%)
  other arithmetic  7.05 us (5%)
  matrix products  6.34 us (4%)
  local copies, waits for them, and re-layouts  6.29 us (4%)
  loops' own time  3.83 us (3%)
    psum x1, blocking collectives, on_device(): spread_sum = lax.psum(jnp.sum(residual * residual), 'samp')  33.9 us
    all_gather x1, waiting for transfers between devices, on_device(): gathered = lax.all_gather(dosages, 'snp', axis=1, tiled=True)  28.2 us
    reduce_scatter x1, waiting for transfers between devices, on_device(): lax.psum_scatter(lax.fori_loop(0, width_slots, one_slot, start_buffer), '...  21.1 us
    all_gather x1, blocking collectives, on_device(): totals = jnp.sum(lax.all_gather(group_part, 'samp'), axis=0)  19.6 us
    unnamed x1, blocking collectives  4.95 us
    dot_general x2, matrix products, one_slot(): jnp.einsum('si,sj->ij', weighted, right, preferred_element_type=jnp.float32)  3.19 us
  transfers between devices with their start and end apart: 2, of which 2 were waited for; matrix products, arithmetic and copies ran while one was open for 3% of the time, Pallas kernels for 0%

profile of v1, /device:TPU:0, one launch (start us, length us, event | category | flops | bytes accessed | tf_op | source)
XLA Modules:
  0.0 146.9 jit_solution(11571138887602071575)
XLA Ops:
  6.5 0.7 all-gather.4.cloned.1.call-update
  7.3 0.8 slice_bitcast_fusion
  8.1 0.9 select_reduce_fusion.1
  9.0 0.9 select_reduce_fusion.4
  9.9 0.8 compare_select_fusion
  10.6 28.2 %all-gather.4.cloned.1.call-done = bf16[768,1024]{1,0:T(8,128)(2,1)} async-done(((bf16[768,512]{1,0:T(8,128)(2,1)}), bf16[768,1024]{1,0:T(8,128)(2,1)}) %all-gather.4.cloned.1.call-update) | async-done | bytes 1572880 | tf_op jit(solution)/shard_map/all_gather | solution.py:18
  38.8 4.9 %while.23 = (s32[]{:T(128)}, bf16[2,768,256]{2,1,0:T(8,128)(2,1)S(1)}, s32[2]{0:T(128)S(1)}, bf16[768,1024]{1,0:T(8,128)(2,1)}, f32[2,768]{1,0:T(2,128)S(1)}, /*...) while((s32[]{:T(128)}, bf16[2,768,256]{2,1,0:T(8,128)(2,1)S(1)}, s32[2]{0:T(128)S(1)}, ...), condition=%wide.region_7.0_spmd, body=%wide.region_6.0_spmd.sunk | while | flops 983046 | bytes 796835 | solution.py:49
  40.1 1.2 fusion.35
  41.3 0.6 dynamic_slice.85
  42.5 1.2 fusion.35
  43.8 11.0 %while.24 = (s32[]{:T(128)}, f32[256,2,2,256]{3,0,1,2:T(8,128)S(1)}, s32[2]{0:T(128)S(1)}, bf16[768,1024]{1,0:T(8,128)(2,1)}, f32[2,768]{1,0:T(2,128)S(1)}, /*in...) while((s32[]{:T(128)}, ...), condition=%wide.region_9.10_spmd, body=%wide.region_8.9_spmd.sunk | while | flops 202637312 | bytes 3155701 | solution.py:68
  43.8 0.6 dynamic_slice.91
  45.0 0.6 dynamic_slice.92
  46.3 1.6 %convolution_bitcast_fusion.5 = f32[256,1,256]{2,0,1:T(8,128)S(1)} fusion(bf16[768,1024]{1,0:T(8,128)(2,1)} %get-tuple-element.320, s32[]{:T(128)S(6)} %select_n.38, f32[768]{0:T(1024)S(1)} %dynamic-slice_reduce_fusion.5, s32[]{:T(128)S(6)} %select_n.37), kind=kOutput, calls=%fused_computation.5.clone.1 | convolution fusion | flops 101253120 | bytes 1051656 | tf_op jit(solution)/shard_map/while/body/eval_jaxpr/si,sj->ij/dot_general | solution.py:61
  47.9 1.3 convolution_bitcast_fusion.4
  50.5 0.6 dynamic_slice.92
  51.7 1.6 %convolution_bitcast_fusion.5 = f32[256,1,256]{2,0,1:T(8,128)S(1)} fusion(bf16[768,1024]{1,0:T(8,128)(2,1)} %get-tuple-element.320, s32[]{:T(128)S(6)} %select_n.38, f32[768]{0:T(1024)S(1)} %dynamic-slice_reduce_fusion.5, s32[]{:T(128)S(6)} %select_n.37), kind=kOutput, calls=%fused_computation.5.clone.1 | convolution fusion | flops 101253120 | bytes 1051656 | tf_op jit(solution)/shard_map/while/body/eval_jaxpr/si,sj->ij/dot_general | solution.py:61
  53.3 1.3 convolution_bitcast_fusion.4
  54.7 1.0 copy-done
  56.4 33.9 %psum.7 = f32[]{:T(128)} all-reduce(f32[]{:T(128)} %multiply_reduce_fusion), channel_id=1, replica_groups=mesh['snp'=2,'samp'=16] {'samp'}, use_global_device_ids=true, to_apply=%region_12.13 | all-reduce | flops 1 | bytes 8 | tf_op jit(solution)/shard_map/psum | solution.py:19
  92.1 21.1 %reduce-scatter.2.cloned.1.call-done = f32[16,2,2,256]{3,0,1,2:T(8,128)} async-done(((f32[256,2,2,256]{3,0,1,2:T(8,128)}), f32[16,2,2,256]{3,0,1,2:T(8,128)}) %reduce-scatter.2.cloned.1.call-update) | async-done | bytes 65552 | tf_op jit(solution)/shard_map/reduce_scatter | solution.py:67
  113.3 0.9 fusion.15
  114.8 4.9 %all-reduce = f32[1024]{0:T(1024)S(1)} all-reduce(f32[1024]{0:T(1024)S(1)} %bitcast.44), channel_id=4, replica_groups=mesh['snp'=2,'samp'=16] {'snp'}, use_global_device_ids=true, to_apply=%region_15.16.clone | all-reduce | flops 1024 | bytes 8192
  119.8 19.6 %all-gather.1 = f32[16,1,512]{2,1,0:T(1,128)S(1)} all-gather(f32[1,1,512]{2,1,0:T(1,128)S(1)} %bitcast.45), channel_id=2, replica_groups=mesh['snp'=2,'samp'=16] {'samp'}, dimensions={0}, use_global_device_ids=true | all-gather | bytes 34816 | tf_op jit(solution)/shard_map/all_gather | solution.py:89
  (30 shorter events, 4.0 us)
Async XLA Ops:
  6.5 32.3 %all-gather.4.cloned.1.call-start = ((), (), s32[]{:S(2)}) async-start(), calls=%async_computation.1 | async-start | bytes 2359296 | tf_op jit(solution)/shard_map/all_gather | solution.py:18
  7.3 106.0 %reduce-scatter.2.cloned.1.call-start = ((), (), s32[]{:S(2)}) async-start(), calls=%async_computation.2 | async-start | bytes 1114112 | tf_op jit(solution)/shard_map/reduce_scatter | solution.py:67
  43.7 12.0 %copy-start.1 = (f32[768]{0:T(1024)S(1)}, f32[768]{0:T(1024)}, u32[]{:S(2)}) copy-start(f32[768]{0:T(1024)} %param.10) | copy-start | bytes 9220
  43.7 47.1 %copy-start.2 = (u32[32]{0:T(128)S(1)}, u32[32]{0:T(128)}, u32[]{:S(2)}) copy-start(u32[32]{0:T(128)} %constant.108) | copy-start | bytes 388
  54.7 1.0 copy-start
Sparse Core Ops, SparseCore 0:
  8.9 29.8 all-gather.3
  55.9 57.3 reduce-scatter.1
